TPU v7x, 128 devices: a whole 4x4x4 slice. The times are simulated.
128 devices in a mesh: island: 8 (over y, x_hi), fsdp: 16 (over z, x_lo, core).
Axes of the slice: x: 4 (x_hi: 2, x_lo: 2; x = x_hi * 2 + x_lo), y: 4, z: 4, core: 2. Of those that a mesh axis runs over, the one named last changes fastest.
Arguments:
- features: bfloat16 [8, 16384, 4096], P('island', 'fsdp'), may hold values from -6 to 6
- upstream: bfloat16 [8, 16384, 1024], P('island', 'fsdp'), may hold values from -0.046875 to 0.046875
- local_weights: float32 [8, 2, 4096, 512], P('island', None, 'fsdp'), may hold values from -6 to 6
- first_moment: float32 [8, 2, 4096, 512], P('island', None, 'fsdp'), may hold values from -4 to 4
- second_moment: float32 [8, 2, 4096, 512], P('island', None, 'fsdp'), may hold values from 0.1 to 1
- anchor: float32 [2, 4096, 512], P(None, 'fsdp'), may hold values from -6 to 6
- outer_momentum: float32 [2, 4096, 512], P(None, 'fsdp'), may hold values from -4 to 4
- fragment: int32 [1], replicated, may hold values from 0 to 7
Outputs:
- weights_out: float32 [8, 2, 4096, 512], P('island', None, 'fsdp')
- first_out: float32 [8, 2, 4096, 512], P('island', None, 'fsdp')
- second_out: float32 [8, 2, 4096, 512], P('island', None, 'fsdp')
- anchor_out: float32 [2, 4096, 512], P(None, 'fsdp')
- momentum_out: float32 [2, 4096, 512], P(None, 'fsdp')
All inputs are finite; a program needn't handle non-finite values.
Results may differ from a plain program's by a relative error of at most 0.0003.
Values may be sent and summed in bfloat16 or wider, within the bound.
A program may use at most 192 MiB of HBM per device.

v0:
```python
import jax
import jax.numpy as jnp
from jax import lax
from jax.sharding import PartitionSpec as P

HEAD = 128


def nesterov(anchor_rows, moment_rows, drift):
    new_moment = 0.9 * moment_rows + drift
    merged = anchor_rows - 0.7 * (0.9 * new_moment + drift)
    return (merged, new_moment)


def body(
    features, upstream, local_weights, first_moment, second_moment, anchor, outer_momentum, fragment
):
    frags = anchor.shape[0]
    kwidth = anchor.shape[2]
    heads = kwidth // HEAD
    index = fragment[0]
    column = index % heads * HEAD
    proj = (jnp.arange(frags) == index // heads)[:, None, None]
    colmask = (jnp.arange(kwidth) // HEAD == index % heads)[None, None, :]
    chosen = jnp.logical_and(proj, colmask)
    anchor_p = jnp.sum(jnp.where(proj, anchor, 0.0), axis=0)
    moment_p = jnp.sum(jnp.where(proj, outer_momentum, 0.0), axis=0)
    own_p = jnp.sum(jnp.where(proj, local_weights[0], 0.0), axis=0)
    anchor_f = lax.dynamic_slice_in_dim(anchor_p, column, HEAD, 1)
    moment_f = lax.dynamic_slice_in_dim(moment_p, column, HEAD, 1)
    own_f = lax.dynamic_slice_in_dim(own_p, column, HEAD, 1)
    difference = anchor_f - own_f
    islands = lax.axis_size("island")
    drift = lax.psum(difference, "island") / islands
    merged, new_moment = nesterov(anchor_f, moment_f, drift)
    merged_p = lax.dynamic_update_slice_in_dim(anchor_p, merged, column, 1)
    moment_new_p = lax.dynamic_update_slice_in_dim(moment_p, new_moment, column, 1)
    momentum_out = jnp.where(chosen, moment_new_p[None], outer_momentum)
    anchor_out = jnp.where(chosen, merged_p[None], anchor)
    start = jnp.where(chosen, merged_p[None], local_weights[0])
    inputs = features[0]
    cotangent = upstream[0]
    contract = (((0,), (0,)), ((), ()))
    term = lax.dot_general(inputs, cotangent, contract, preferred_element_type=jnp.float32)
    grad = lax.psum_scatter(term, "fsdp", scatter_dimension=0, tiled=True)
    owned = grad.shape[0]
    grad = grad.reshape(owned, frags, grad.shape[1] // frags).transpose(1, 0, 2)
    first_new = 0.9 * first_moment[0] + 0.1 * grad
    second_new = 0.95 * second_moment[0] + 0.05 * grad * grad
    weights_new = start - 0.02 * (first_new / (jnp.sqrt(second_new) + 1e-08) + 0.1 * start)
    return (weights_new[None], first_new[None], second_new[None], anchor_out, momentum_out)


def solution(mesh):
    placed = (
        P("island", "fsdp", None),
        P("island", "fsdp", None),
        P("island", None, "fsdp", None),
        P("island", None, "fsdp", None),
        P("island", None, "fsdp", None),
        P(None, "fsdp", None),
        P(None, "fsdp", None),
        P(),
    )
    return jax.shard_map(
        body,
        mesh=mesh,
        in_specs=placed,
        out_specs=(
            P("island", None, "fsdp", None),
            P("island", None, "fsdp", None),
            P("island", None, "fsdp", None),
            P(None, "fsdp", None),
            P(None, "fsdp", None),
        ),
        check_vma=False,
    )
```

profile of v0, /device:TPU:0, one launch (start us, length us, event | category | flops | bytes accessed | tf_op | source)
XLA Modules:
  0.0 230.2 jit_solution(9732067150084903960)
XLA Ops:
  8.0 0.0 copy-start
  8.0 0.0 all-reduce.2.cloned.1.call-start
  8.9 3.4 %select_reduce_fusion = (f32[256,512]{1,0:T(8,128)}, f32[256,512]{1,0:T(8,128)S(1)}, f32[256,512]{1,0:T(8,128)S(1)}) fusion(f32[2,256,512]{2,1,0:T(8,128)} %param.14, pred[2]{0:T(512)(128)(4,1)S(1)} %iota_compare_fusion, f32[1,2,256,512]{3,2,1,0:T(8,128)} %param.10, f32[2,256,512]{2,1,0:T(8,128)} %param.13), kind=kLoop, calls=%fused_computation.12 | loop fusion | flops 1179648 | bytes 4718594 | tf_op jit(solution)/shard_map/reduce_sum | solution.py:27
  12.3 0.0 copy-start.2
  12.3 0.8 copy-done.2
  13.1 0.7 dynamic-slice_subtract_fusion
  13.8 0.0 all-reduce.2.cloned.1.call-update
  13.8 0.0 reduce-scatter.2.cloned.1.call-start
  13.8 0.0 copy-done
  13.9 14.6 %fusion = f32[4096,1024]{1,0:T(8,128)} fusion(bf16[1,1024,4096]{2,1,0:T(8,128)(2,1)} %param.8, bf16[1,1024,1024]{2,1,0:T(8,128)(2,1)S(1)} %copy-done), kind=kOutput, calls=%fused_computation | convolution fusion | flops 8589934592 | bytes 27262976 | tf_op jit(solution)/shard_map/dot_general | solution.py:44
  28.4 0.0 copy-start.1
  28.4 0.0 reduce-scatter.2.cloned.1.call-update
  28.5 0.1 broadcast_and_fusion
  28.5 147.4 %all-reduce.2.cloned.1.call-done = f32[256,128]{1,0:T(8,128)} async-done(((f32[256,128]{1,0:T(8,128)}), f32[256,128]{1,0:T(8,128)}) %all-reduce.2.cloned.1.call-update) | async-done | bytes 131088 | tf_op jit(solution)/shard_map/psum | solution.py:34
  175.9 1.8 fusion.9
  177.7 39.2 %reduce-scatter.2.cloned.1.call-done = f32[256,1024]{1,0:T(8,128)} async-done(((f32[4096,1024]{1,0:T(8,128)}), f32[256,1024]{1,0:T(8,128)}) %reduce-scatter.2.cloned.1.call-update) | async-done | bytes 1048592 | tf_op jit(solution)/shard_map/reduce_scatter | solution.py:45
  216.9 0.0 copy-done.1
  216.9 5.9 %fusion.8 = (f32[1,2,256,512]{3,2,1,0:T(8,128)}, f32[1,2,256,512]{3,2,1,0:T(8,128)}, f32[1,2,256,512]{3,2,1,0:T(8,128)}, f32[2,256,512]{2,1,0:T(8,128)}, f32[2,256,512]{2,1,0:T(8,128)}) fusion(f32[32,2,8,512]{3,2,1,0:T(8,128)} %bitcast.69, f32[1,2,256,512]{3,2,1,0:T(8,128)} %param.12, f32[1,2,256,512]{3,2,1,0:T(8,128)} %param.11, ...), kind=kLoop, calls=%fused_computation.17 | loop fusion | flops 4194304 | bytes 12583936 | tf_op jit(solution)/shard_map/broadcast_in_dim | solution.py:51
  (2 shorter events, 0.0 us)
Async XLA Ops:
  8.0 5.8 %copy-start = (bf16[1,1024,1024]{2,1,0:T(8,128)(2,1)S(1)}, bf16[1,1024,1024]{2,1,0:T(8,128)(2,1)}, u32[]{:S(2)}) copy-start(bf16[1,1024,1024]{2,1,0:T(8,128)(2,1)} %param.9) | copy-start | bytes 6291460
  8.0 167.9 %all-reduce.2.cloned.1.call-start = ((), (), s32[]{:S(2)}) async-start(), calls=%async_computation.1 | async-start | bytes 262144 | tf_op jit(solution)/shard_map/psum | solution.py:34
  12.3 0.8 copy-start.2
  13.8 203.1 %reduce-scatter.2.cloned.1.call-start = ((), (), s32[]{:S(2)}) async-start(), calls=%async_computation.2 | async-start | bytes 17825792 | tf_op jit(solution)/shard_map/reduce_scatter | solution.py:45
  28.4 188.5 %copy-start.1 = (f32[1,2,256,512]{3,2,1,0:T(8,128)S(1)}, f32[1,2,256,512]{3,2,1,0:T(8,128)}, u32[]{:S(2)}) copy-start(f32[1,2,256,512]{3,2,1,0:T(8,128)} %param.10) | copy-start | bytes 3145732
Sparse Core Ops, SparseCore 0:
  13.9 161.9 all-reduce.1
Sparse Core Ops, SparseCore 1:
  28.5 188.3 reduce-scatter.1
where the time goes:
time: 230 us
  waiting for transfers between devices  187 us (81%)
  between operations  16.3 us (7%)
  matrix products  14.6 us (6%)
  other arithmetic  11.8 us (5%)
    psum x1, waiting for transfers between devices, body(): drift = lax.psum(difference, 'island') / islands  147 us
    reduce_scatter x1, waiting for transfers between devices, body(): grad = lax.psum_scatter(term, 'fsdp', scatter_dimension=0, tiled=True)  39.2 us
    dot_general x1, matrix products, body(): lax.dot_general(inputs, cotangent, contract, preferred_element_type=jnp.f...  14.6 us
    broadcast_in_dim x1, other arithmetic, body(): second_new[None]  5.87 us
  transfers between devices with their start and end apart: 2, of which 2 were waited for; matrix products, arithmetic and copies ran while one was open for 7% of the time, Pallas kernels for 0%

commit v1 on v0

v1 whole, which is shorter than its diff:
```python
import functools

import jax
import jax.numpy as jnp
from jax import lax
from jax.experimental import pallas as pl
from jax.experimental.pallas import tpu as pltpu
from jax.sharding import PartitionSpec as P

HEAD = 128
LANES = 128
TOP = 32766.0
TINY = 1e-30
F32 = jnp.float32
MESH = pl.DeviceIdType.MESH


def encode(value, codes, scales):
    @pl.loop(0, codes.shape[1] // LANES)
    def _(j):
        lanes = pl.ds(pl.multiple_of(j * LANES, LANES), LANES)
        v = value(lanes)
        top = jnp.maximum(jnp.max(jnp.abs(v), axis=0, keepdims=True), TINY)
        scales[:, lanes] = top * (1.0 / TOP)
        codes[:, lanes] = jnp.round(v * (TOP / top)).astype(jnp.int32).astype(jnp.int16)


def decode(codes, scales, lanes):
    return codes[:, lanes].astype(jnp.int32).astype(F32) * scales[:, lanes]


def grad_kernel(
    rows, zrows, x_hbm, u_hbm, lw_hbm, frag, grad, total,
    xb, ub, lwb, part, own, core_in,
    zq, zs, zq_in, zs_in, wq, ws, wq_in, ws_in,
    xq, xs, xq_in, xs_in, yq, ys, yq_in, ys_in,
    mine, slots, half_sum, half_in,
    load_sem, core_ss, core_rs, z_ss, z_rs, w_ss, w_rs, x_ss, x_rs, y_ss, y_rs, d_ss, d_rs,
):
    isl, place = lax.axis_index("island"), lax.axis_index("fsdp")
    z, x, c = place // 4, place // 2 % 2, place % 2
    y, h = isl // 2, isl % 2
    half = grad.shape[2]
    quarter = rows // 4

    def at(dz=0, dx=0, dc=0):
        return (isl, (z + dz) % 4 * 4 + (x + dx) % 2 * 2 + (c + dc) % 2)

    def island(dy=0, dh=0):
        return ((y + dy) % 4 * 2 + (h + dh) % 2, place)

    def order(k):
        dz = jnp.where(k < 2, 2, jnp.where(k >= 6, 0, jnp.where(k % 2 == 0, 1, 3)))
        dx = jnp.where(k < 2, 1 - k, jnp.where(k < 4, 1, jnp.where(k < 6, 0, 7 - k)))
        return (z + dz) % 4 * 2 + (x + dx) % 2

    def load_x(k):
        chip = pl.ds(pl.multiple_of(order(k) * 2 * rows, 2 * rows), 2 * rows)
        return pltpu.make_async_copy(x_hbm.at[0, :, chip], xb.at[:, chip], load_sem.at[k])

    load_u = pltpu.make_async_copy(u_hbm.at[0], ub, load_sem.at[8])
    load_lw = pltpu.make_async_copy(lw_hbm.at[0], lwb, load_sem.at[9])
    load_u.start()

    @pl.loop(0, 8)
    def _(k):
        load_x(k).start()

    load_lw.start()

    barrier = pltpu.get_barrier_semaphore()
    peers = [at(dc=1), at(dx=1), at(dz=1), at(dz=3), island(1), island(2), island(3), island(dh=1)]
    for peer in peers:
        pl.semaphore_signal(barrier, inc=1, device_id=peer, device_id_type=MESH)

    def remote(src, dst, ss, rs, peer):
        return pltpu.make_async_remote_copy(
            src_ref=src, dst_ref=dst, send_sem=ss, recv_sem=rs, device_id=peer, device_id_type=MESH
        )

    def term(k, core):
        offset = pl.multiple_of((order(k) * 2 + core) * rows, rows)
        return lax.dot_general(
            xb[:, pl.ds(offset, rows)], ub[...], (((0,), (0,)), ((), ())), preferred_element_type=F32
        )

    def core_copy(k):
        return remote(part.at[k], core_in.at[k], core_ss.at[k], core_rs.at[k], at(dc=1))

    def z_copy(d, s):
        peer = at(dz=1 if d == 0 else 3)
        return (
            remote(zq.at[d, s], zq_in.at[d, s], z_ss.at[d, s, 0], z_rs.at[d, s, 0], peer),
            remote(zs.at[d, s], zs_in.at[d, s], z_ss.at[d, s, 1], z_rs.at[d, s, 1], peer),
        )

    def w_copy(d, s):
        peer = at(dz=1 if d == 0 else 3)
        return (
            remote(wq.at[d, s], wq_in.at[d, s], w_ss.at[d, s, 0], w_rs.at[d, s, 0], peer),
            remote(ws.at[d, s], ws_in.at[d, s], w_ss.at[d, s, 1], w_rs.at[d, s, 1], peer),
        )

    def x_copy(s):
        peer = at(dx=1)
        return (
            remote(xq.at[s], xq_in.at[s], x_ss.at[s, 0], x_rs.at[s, 0], peer),
            remote(xs.at[s], xs_in.at[s], x_ss.at[s, 1], x_rs.at[s, 1], peer),
        )

    def y_copy():
        peer = at(dx=1)
        return (
            remote(yq, yq_in, y_ss.at[0], y_rs.at[0], peer),
            remote(ys, ys_in, y_ss.at[1], y_rs.at[1], peer),
        )

    def start(pair):
        for copy in pair:
            copy.start()

    def arrive(pair):
        for copy in pair:
            copy.wait_recv()

    def shifted(lanes, columns):
        return pl.ds(pl.multiple_of(lanes.start + columns, LANES), LANES)

    def chip_term(k, r, n, side=0):
        def value(lanes):
            lanes = shifted(lanes, side * half)
            return own[k, pl.ds(r, n), lanes] + core_in[k, pl.ds(r, n), lanes]

        return value

    wrows = rows - zrows

    def z_term(k, side):
        return chip_term(k, 0, zrows, side)

    def w_term(k, slot, side):
        base = chip_term(k, zrows, wrows, side)

        def value(lanes):
            return base(lanes) + decode(xq_in.at[slot], xs_in.at[slot], shifted(lanes, side * half))

        return value

    def send_z(d, s, value):
        encode(value, zq.at[d, s], zs.at[d, s])
        start(z_copy(d, s))

    def send_w(d, s, value):
        encode(value, wq.at[d, s], ws.at[d, s])
        start(w_copy(d, s))

    def send_x(s, k):
        encode(chip_term(k, zrows, wrows), xq.at[s], xs.at[s])
        start(x_copy(s))

    def z_plus(d, k, got):
        arrive(z_copy(d, got))
        return lambda lanes: z_term(k, d)(lanes) + decode(zq_in.at[d, got], zs_in.at[d, got], lanes)

    load_u.wait()

    @pl.loop(0, 2)
    def _(k):
        load_x(k).wait()
        part[k] = term(k, 1 - c)

        @pl.when(k == 0)
        def _():
            pl.semaphore_wait(barrier, len(peers))

        core_copy(k).start()

    load_lw.wait()
    index = frag[0]
    heads = half // HEAD

    @pl.loop(0, rows // 32)
    def _(j):
        few = pl.ds(pl.multiple_of(j * 32, 32), 32)
        chosen = lwb[0, few, pl.ds(0, HEAD)]
        for g in range(1, heads * lwb.shape[0]):
            chosen = jnp.where(index == g, lwb[g // heads, few, pl.ds(g % heads * HEAD, HEAD)], chosen)
        mine[few, :] = chosen

    def y_rows(dy):
        return pl.ds(pl.multiple_of((y + dy) % 4 * quarter, quarter), quarter)

    def scatter_copy(dy):
        return remote(mine.at[y_rows(dy)], slots.at[dy - 1], d_ss.at[dy - 1], d_rs.at[dy - 1], island(dy))

    def cross_copy():
        return remote(half_sum, half_in, d_ss.at[3], d_rs.at[3], island(dh=1))

    def gather_copy(dy):
        return remote(total.at[y_rows(0)], total.at[y_rows(0)], d_ss.at[3 + dy], d_rs.at[3 + dy], island(dy))

    def gather_arrive(dy):
        rows_in = total.at[y_rows(-dy)]
        return remote(rows_in, rows_in, d_ss.at[3 + dy], d_rs.at[3 + dy], island(dy))

    for dy in (1, 2, 3):
        scatter_copy(dy).start()

    @pl.loop(0, 8)
    def _(k):
        own[k] = term(k, c)

        @pl.when(k < 6)
        def _():
            load_x(k + 2).wait()
            part[k + 2] = term(k + 2, 1 - c)
            core_copy(k + 2).start()

        core_copy(k).wait_recv()

        @pl.when(k == 0)
        def _():
            send_z(0, 0, z_term(0, 0))
            send_z(1, 0, z_term(0, 1))
            send_x(0, 0)

        @pl.when(k == 1)
        def _():
            send_z(0, 1, z_term(1, 0))
            send_z(1, 1, z_term(1, 1))

        @pl.when(k == 2)
        def _():
            send_x(1, 2)
            send_z(0, 2, z_term(2, 1))
            for dy in (1, 2, 3):
                scatter_copy(dy).wait_recv()
            half_sum[...] = mine[y_rows(0), :] + slots[0] + slots[1] + slots[2]
            cross_copy().start()

        @pl.when(k == 3)
        def _():
            send_x(2, 3)
            send_z(1, 2, z_term(3, 0))

        @pl.when(k == 4)
        def _():
            send_z(0, 3, z_plus(0, 2, 0))
            send_z(1, 3, z_plus(1, 3, 0))
            send_z(0, 4, z_term(4, 1))
            cross_copy().wait_recv()
            total[y_rows(0), :] = half_sum[...] + half_in[...]
            for dy in (1, 2, 3):
                gather_copy(dy).start()

        @pl.when(k == 5)
        def _():
            send_z(1, 4, z_term(5, 0))

        @pl.when(k == 6)
        def _():
            send_x(3, 6)

    send_z(0, 5, z_plus(0, 4, 1))
    send_z(1, 5, z_plus(1, 5, 1))

    arrive(x_copy(0))
    send_w(0, 0, w_term(1, 0, 0))
    send_w(1, 0, w_term(1, 0, 1))

    def z_sum(k, leaf, chain, side):
        def value(lanes):
            return (
                z_term(k, side)(lanes)
                + decode(zq_in.at[side, chain], zs_in.at[side, chain], lanes)
                + decode(zq_in.at[1 - side, leaf], zs_in.at[1 - side, leaf], lanes)
            )

        return value

    for d in (0, 1):
        arrive(z_copy(d, 2))
        arrive(z_copy(d, 3))
    for side in (0, 1):
        columns = pl.ds(side * half, half)
        encode(z_sum(6, 2, 3, side), yq.at[:, columns], ys.at[:, columns])
    start(y_copy())

    arrive(x_copy(1))
    send_w(0, 1, w_term(4, 1, 1))
    arrive(x_copy(2))
    send_w(1, 1, w_term(5, 2, 0))
    for d, k, slot in ((0, 4, 1), (1, 5, 2)):
        arrive(w_copy(d, 0))
        base = w_term(k, slot, d)
        send_w(d, 2, lambda lanes, d=d, base=base: base(lanes) + decode(wq_in.at[d, 0], ws_in.at[d, 0], lanes))

    for d in (0, 1):
        arrive(z_copy(d, 4))
        arrive(z_copy(d, 5))
    arrive(x_copy(3))
    arrive(y_copy())
    for side in (0, 1):
        base = z_sum(7, 4, 5, side)

        @pl.loop(0, half // LANES)
        def _(j):
            lanes = pl.ds(pl.multiple_of(j * LANES, LANES), LANES)
            grad[side, pl.ds(0, zrows), lanes] = base(lanes) + decode(yq_in, ys_in, shifted(lanes, side * half))

    for d in (0, 1):
        arrive(w_copy(d, 1))
        arrive(w_copy(d, 2))
    for side in (0, 1):
        base = w_term(7, 3, side)

        @pl.loop(0, half // LANES)
        def _(j):
            lanes = pl.ds(pl.multiple_of(j * LANES, LANES), LANES)
            grad[side, pl.ds(zrows, wrows), lanes] = (
                base(lanes)
                + decode(wq_in.at[side, 2], ws_in.at[side, 2], lanes)
                + decode(wq_in.at[1 - side, 1], ws_in.at[1 - side, 1], lanes)
            )

    for dy in (1, 2, 3):
        gather_arrive(dy).wait_recv()
        gather_copy(dy).wait_send()
        scatter_copy(dy).wait_send()
    cross_copy().wait_send()

    @pl.loop(0, 8)
    def _(k):
        core_copy(k).wait_send()

    pairs = [z_copy(d, s) for d in (0, 1) for s in range(6)] + [w_copy(d, s) for d in (0, 1) for s in range(3)]
    pairs += [x_copy(s) for s in range(4)] + [y_copy()]
    for pair in pairs:
        for copy in pair:
            copy.wait_send()


def update_kernel(
    islands, frag, grad, total, lw, first, second, anchor, moment, lw_out, first_out, second_out, anchor_out, moment_out
):
    index = frag[0]
    heads = lw.shape[3] // HEAD
    proj, column = index // heads, pl.multiple_of(index % heads * HEAD, HEAD)
    anchor_f = anchor[proj, :, pl.ds(column, HEAD)]
    moment_f = moment[proj, :, pl.ds(column, HEAD)]
    drift = anchor_f - total[...] * (1.0 / islands)
    moment_new = 0.9 * moment_f + drift
    merged = anchor_f - 0.7 * (0.9 * moment_new + drift)
    for p in range(lw.shape[1]):
        for j in range(heads):
            here = index == p * heads + j
            lanes = pl.ds(j * HEAD, HEAD)
            anchor_out[p, :, lanes] = jnp.where(here, merged, anchor[p, :, lanes])
            moment_out[p, :, lanes] = jnp.where(here, moment_new, moment[p, :, lanes])
            begin = jnp.where(here, merged, lw[0, p, :, lanes])
            g = grad[p, :, lanes]
            m = 0.9 * first[0, p, :, lanes] + 0.1 * g
            v = 0.95 * second[0, p, :, lanes] + 0.05 * g * g
            first_out[0, p, :, lanes] = m
            second_out[0, p, :, lanes] = v
            lw_out[0, p, :, lanes] = begin - 0.02 * (m / (jnp.sqrt(v) + 1e-08) + 0.1 * begin)


def body(features, upstream, local_weights, first_moment, second_moment, anchor, outer_momentum, fragment):
    _, tokens, width = features.shape
    _, frags, rows, half = local_weights.shape
    cols = frags * half
    zrows = rows * 9 // 16
    wrows = rows - zrows
    i16 = jnp.int16

    def vm(shape, dtype):
        return pltpu.VMEM(shape, dtype)

    def both(*shape):
        return [vm(shape, i16), vm(shape[:-2] + (1, shape[-1]), F32)] * 2

    def sems(*shape):
        return pltpu.SemaphoreType.DMA(shape)

    any_space = pl.BlockSpec(memory_space=pl.ANY)
    grad, total = pl.pallas_call(
        functools.partial(grad_kernel, rows, zrows),
        out_shape=(
            jax.ShapeDtypeStruct((frags, rows, half), F32),
            jax.ShapeDtypeStruct((rows, HEAD), F32),
        ),
        in_specs=[any_space, any_space, any_space, pl.BlockSpec(memory_space=pltpu.SMEM)],
        out_specs=(pl.BlockSpec(memory_space=pltpu.VMEM), pl.BlockSpec(memory_space=pltpu.VMEM)),
        scratch_shapes=[
            vm((tokens, width), jnp.bfloat16),
            vm((tokens, cols), jnp.bfloat16),
            vm((frags, rows, half), F32),
            vm((8, rows, cols), F32),
            vm((8, rows, cols), F32),
            vm((8, rows, cols), F32),
            *both(2, 6, zrows, half),
            *both(2, 3, wrows, half),
            *both(4, wrows, cols),
            *both(zrows, cols),
            vm((rows, HEAD), F32),
            vm((3, rows // 4, HEAD), F32),
            vm((rows // 4, HEAD), F32),
            vm((rows // 4, HEAD), F32),
            sems(10),
            sems(8),
            sems(8),
            sems(2, 6, 2),
            sems(2, 6, 2),
            sems(2, 3, 2),
            sems(2, 3, 2),
            sems(4, 2),
            sems(4, 2),
            sems(2),
            sems(2),
            sems(7),
            sems(7),
        ],
        compiler_params=pltpu.CompilerParams(
            collective_id=0, has_side_effects=True, vmem_limit_bytes=56 * 2**20
        ),
    )(features, upstream, local_weights, fragment)

    step = rows // 4
    state = pl.BlockSpec((1, frags, step, half), lambda i: (0, 0, i, 0))
    shared = pl.BlockSpec((frags, step, half), lambda i: (0, i, 0))
    weights_shape = jax.ShapeDtypeStruct(local_weights.shape, F32)
    anchor_shape = jax.ShapeDtypeStruct(anchor.shape, F32)
    return pl.pallas_call(
        functools.partial(update_kernel, lax.axis_size("island")),
        grid=(4,),
        out_shape=(weights_shape, weights_shape, weights_shape, anchor_shape, anchor_shape),
        in_specs=[
            pl.BlockSpec(memory_space=pltpu.SMEM),
            shared,
            pl.BlockSpec((step, HEAD), lambda i: (i, 0)),
            state,
            state,
            state,
            shared,
            shared,
        ],
        out_specs=(state, state, state, shared, shared),
        compiler_params=pltpu.CompilerParams(vmem_limit_bytes=16 * 2**20),
    )(fragment, grad, total, local_weights, first_moment, second_moment, anchor, outer_momentum)


def solution(mesh):
    placed = (
        P("island", "fsdp", None),
        P("island", "fsdp", None),
        P("island", None, "fsdp", None),
        P("island", None, "fsdp", None),
        P("island", None, "fsdp", None),
        P(None, "fsdp", None),
        P(None, "fsdp", None),
        P(),
    )
    return jax.shard_map(
        body,
        mesh=mesh,
        in_specs=placed,
        out_specs=(
            P("island", None, "fsdp", None),
            P("island", None, "fsdp", None),
            P("island", None, "fsdp", None),
            P(None, "fsdp", None),
            P(None, "fsdp", None),
        ),
        check_vma=False,
    )
```

time: 230 us -> 53.3 us (0.23)
  waiting for transfers between devices: 187 us -> 0 us
  Pallas kernels: 0 us -> 48.7 us
  between operations: 16.3 us -> 1.53 us
  matrix products: 14.6 us -> 0 us
  other arithmetic: 11.8 us -> 0 us
    psum x1 -> x0, waiting for transfers between devices: 147 us -> none  [body(): drift = lax.psum(difference, 'island') / islands]
    pallas_call x0 -> x2, Pallas kernels: none -> 48.7 us  [the longest x1 45.2 us: body(): pl.pallas_call(functools.partial(grad_kernel, rows, zrows), out_shape=(ja...]
    reduce_scatter x1 -> x0, waiting for transfers between devices: 39.2 us -> none  [body(): grad = lax.psum_scatter(term, 'fsdp', scatter_dimension=0, tiled=True)]
    dot_general x1 -> x0, matrix products: 14.6 us -> none  [body(): lax.dot_general(inputs, cotangent, contract, preferred_element_type=jnp.f...]
    broadcast_in_dim x1 -> x0, other arithmetic: 5.87 us -> none  [body(): second_new[None]]
    reduce_sum x1 -> x0, other arithmetic: 3.36 us -> none  [body(): moment_p = jnp.sum(jnp.where(proj, outer_momentum, 0.0), axis=0)]
  transfers between devices with their start and end apart: 2 -> 0, of which waited for: 2 -> 0; matrix products, arithmetic and copies ran while one was open for 7% -> 0% of each run, Pallas kernels for 0% -> 0%
where the time goes in v1:
time: 53.3 us; the launch traced here: 52.4 us
  Pallas kernels  48.7 us (91%)
  local copies, waits for them, and re-layouts  2.14 us (4%)
  between operations  1.53 us (3%)
    pallas_call x1, Pallas kernels, body(): pl.pallas_call(functools.partial(grad_kernel, rows, zrows), out_shape=(ja...  45.2 us
    pallas_call x1, Pallas kernels, body(): pl.pallas_call(functools.partial(update_kernel, lax.axis_size('island')),...  3.45 us
    unnamed x14, local copies, waits for them, and re-layouts  2.14 us

profile of v1, /device:TPU:0, one launch (start us, length us, event | category | flops | bytes accessed | tf_op | source)
XLA Modules:
  0.0 52.4 jit_solution(10720721114461928082)
XLA Ops:
  0.6 0.0 copy-start
  0.6 0.0 copy-start.4
  0.7 0.0 copy-start.3
  0.7 0.0 copy-start.2
  0.7 0.0 copy-start.1
  1.5 45.2 %shard_map.119 = (f32[2,256,512]{2,1,0:T(8,128)}, f32[256,128]{1,0:T(8,128)}) custom-call(bf16[1,1024,4096]{2,1,0:T(8,128)(2,1)} %x_hbm.1, bf16[1,1024,1024]{2,1,0:T(8,128)(2,1)} %u_hbm.1, f32[1,2,256,512]{3,2,1,0:T(8,128)} %lw.1, s32[1]{0:T(128)S(6)} %copy.13.frag), custom_call_target="tpu_custom_call" | custom-call | tf_op jit(solution)/shard_map/pallas_call | solution.py:387
  46.7 0.0 copy-done
  46.7 0.0 copy-done.4
  46.7 0.0 copy-done.3
  46.8 0.0 copy-done.2
  46.8 0.0 copy-done.1
  46.8 0.0 copy-start.5
  46.8 1.2 %copy-done.5 = f32[2,256,512]{2,1,0:T(8,128)S(1)} copy-done((f32[2,256,512]{2,1,0:T(8,128)S(1)}, f32[2,256,512]{2,1,0:T(8,128)}, u32[]{:S(2)}) %copy-start.5) | copy-done | bytes 1048600
  48.0 0.0 copy-start.6
  48.0 0.9 %copy-done.6 = f32[256,128]{1,0:T(8,128)S(1)} copy-done((f32[256,128]{1,0:T(8,128)S(1)}, f32[256,128]{1,0:T(8,128)}, u32[]{:S(2)}) %copy-start.6) | copy-done | bytes 131096
  48.9 3.4 %shard_map.120 = (f32[1,2,256,512]{3,2,1,0:T(8,128)}, f32[1,2,256,512]{3,2,1,0:T(8,128)}, f32[1,2,256,512]{3,2,1,0:T(8,128)}, f32[2,256,512]{2,1,0:T(8,128)}, f32[2,256,512]{2,1,0:T(8,128)}) custom-call(s32[1]{0:T(128)S(6)} %copy.13.frag, f32[2,256,512]{2,1,0:T(8,128)S(1)} %copy-done.5, f32[256,128]{1,0:T(8,128)S(1)} %copy-done.6, ...), custom_call_target="tpu_custom_call" | custom-call | tf_op jit(solution)/shard_map/pallas_call | solution.py:434
Async XLA Ops:
  0.6 46.1 %copy-start = (f32[1,2,256,512]{3,2,1,0:T(8,128)S(1)}, f32[1,2,256,512]{3,2,1,0:T(8,128)}, u32[]{:S(2)}) copy-start(f32[1,2,256,512]{3,2,1,0:T(8,128)} %lw.1) | copy-start | bytes 3145732
  0.6 46.1 %copy-start.4 = (f32[2,256,512]{2,1,0:T(8,128)S(1)}, f32[2,256,512]{2,1,0:T(8,128)}, u32[]{:S(2)}) copy-start(f32[2,256,512]{2,1,0:T(8,128)} %moment.1) | copy-start | bytes 3145732
  0.7 46.1 %copy-start.3 = (f32[2,256,512]{2,1,0:T(8,128)S(1)}, f32[2,256,512]{2,1,0:T(8,128)}, u32[]{:S(2)}) copy-start(f32[2,256,512]{2,1,0:T(8,128)} %anchor.1) | copy-start | bytes 3145732
  0.7 46.1 %copy-start.2 = (f32[1,2,256,512]{3,2,1,0:T(8,128)S(1)}, f32[1,2,256,512]{3,2,1,0:T(8,128)}, u32[]{:S(2)}) copy-start(f32[1,2,256,512]{3,2,1,0:T(8,128)} %second.1) | copy-start | bytes 3145732
  0.7 46.1 %copy-start.1 = (f32[1,2,256,512]{3,2,1,0:T(8,128)S(1)}, f32[1,2,256,512]{3,2,1,0:T(8,128)}, u32[]{:S(2)}) copy-start(f32[1,2,256,512]{3,2,1,0:T(8,128)} %first.1) | copy-start | bytes 3145732
  46.8 1.2 %copy-start.5 = (f32[2,256,512]{2,1,0:T(8,128)S(1)}, f32[2,256,512]{2,1,0:T(8,128)}, u32[]{:S(2)}) copy-start(f32[2,256,512]{2,1,0:T(8,128)} %get-tuple-element.7.grad) | copy-start | bytes 3145732
  48.0 0.9 %copy-start.6 = (f32[256,128]{1,0:T(8,128)S(1)}, f32[256,128]{1,0:T(8,128)}, u32[]{:S(2)}) copy-start(f32[256,128]{1,0:T(8,128)} %get-tuple-element.8.total) | copy-start | bytes 393220

commit v2 on v1

--- a/solution.py
+++ b/solution.py
@@ -30,8 +30,9 @@
 
 
 def grad_kernel(
-    rows, zrows, x_hbm, u_hbm, lw_hbm, frag, grad, total,
-    xb, ub, lwb, part, own, core_in,
+    rows, zrows, x_hbm, u_hbm, lw_hbm, first_hbm, second_hbm, anchor_hbm, moment_hbm, frag,
+    grad, total, lwb, firstb, secondb, anchorb, momentb,
+    xb, ub, part, own, core_in,
     zq, zs, zq_in, zs_in, wq, ws, wq_in, ws_in,
     xq, xs, xq_in, xs_in, yq, ys, yq_in, ys_in,
     mine, slots, half_sum, half_in,
@@ -59,7 +60,9 @@
         return pltpu.make_async_copy(x_hbm.at[0, :, chip], xb.at[:, chip], load_sem.at[k])
 
     load_u = pltpu.make_async_copy(u_hbm.at[0], ub, load_sem.at[8])
-    load_lw = pltpu.make_async_copy(lw_hbm.at[0], lwb, load_sem.at[9])
+    load_lw = pltpu.make_async_copy(lw_hbm, lwb, load_sem.at[9])
+    rest = ((first_hbm, firstb), (second_hbm, secondb), (anchor_hbm, anchorb), (moment_hbm, momentb))
+    load_rest = [pltpu.make_async_copy(src, dst, load_sem.at[10 + n]) for n, (src, dst) in enumerate(rest)]
     load_u.start()
 
     @pl.loop(0, 8)
@@ -182,9 +185,9 @@
     @pl.loop(0, rows // 32)
     def _(j):
         few = pl.ds(pl.multiple_of(j * 32, 32), 32)
-        chosen = lwb[0, few, pl.ds(0, HEAD)]
-        for g in range(1, heads * lwb.shape[0]):
-            chosen = jnp.where(index == g, lwb[g // heads, few, pl.ds(g % heads * HEAD, HEAD)], chosen)
+        chosen = lwb[0, 0, few, pl.ds(0, HEAD)]
+        for g in range(1, heads * lwb.shape[1]):
+            chosen = jnp.where(index == g, lwb[0, g // heads, few, pl.ds(g % heads * HEAD, HEAD)], chosen)
         mine[few, :] = chosen
 
     def y_rows(dy):
@@ -205,68 +208,8 @@
 
     for dy in (1, 2, 3):
         scatter_copy(dy).start()
-
-    @pl.loop(0, 8)
-    def _(k):
-        own[k] = term(k, c)
-
-        @pl.when(k < 6)
-        def _():
-            load_x(k + 2).wait()
-            part[k + 2] = term(k + 2, 1 - c)
-            core_copy(k + 2).start()
-
-        core_copy(k).wait_recv()
-
-        @pl.when(k == 0)
-        def _():
-            send_z(0, 0, z_term(0, 0))
-            send_z(1, 0, z_term(0, 1))
-            send_x(0, 0)
-
-        @pl.when(k == 1)
-        def _():
-            send_z(0, 1, z_term(1, 0))
-            send_z(1, 1, z_term(1, 1))
-
-        @pl.when(k == 2)
-        def _():
-            send_x(1, 2)
-            send_z(0, 2, z_term(2, 1))
-            for dy in (1, 2, 3):
-                scatter_copy(dy).wait_recv()
-            half_sum[...] = mine[y_rows(0), :] + slots[0] + slots[1] + slots[2]
-            cross_copy().start()
-
-        @pl.when(k == 3)
-        def _():
-            send_x(2, 3)
-            send_z(1, 2, z_term(3, 0))
-
-        @pl.when(k == 4)
-        def _():
-            send_z(0, 3, z_plus(0, 2, 0))
-            send_z(1, 3, z_plus(1, 3, 0))
-            send_z(0, 4, z_term(4, 1))
-            cross_copy().wait_recv()
-            total[y_rows(0), :] = half_sum[...] + half_in[...]
-            for dy in (1, 2, 3):
-                gather_copy(dy).start()
-
-        @pl.when(k == 5)
-        def _():
-            send_z(1, 4, z_term(5, 0))
-
-        @pl.when(k == 6)
-        def _():
-            send_x(3, 6)
-
-    send_z(0, 5, z_plus(0, 4, 1))
-    send_z(1, 5, z_plus(1, 5, 1))
-
-    arrive(x_copy(0))
-    send_w(0, 0, w_term(1, 0, 0))
-    send_w(1, 0, w_term(1, 0, 1))
+    for copy in load_rest:
+        copy.start()
 
     def z_sum(k, leaf, chain, side):
         def value(lanes):
@@ -278,6 +221,80 @@
 
         return value
 
+    def collect(side, r, n, value):
+        @pl.loop(0, half // LANES)
+        def _(j):
+            lanes = pl.ds(pl.multiple_of(j * LANES, LANES), LANES)
+            grad[side, pl.ds(r, n), lanes] = value(lanes)
+
+    def add(side, r, n, value):
+        @pl.loop(0, half // LANES)
+        def _(j):
+            lanes = pl.ds(pl.multiple_of(j * LANES, LANES), LANES)
+            grad[side, pl.ds(r, n), lanes] += value(lanes)
+
+    @pl.loop(0, 8)
+    def _(k):
+        own[k] = term(k, c)
+
+        @pl.when(k < 6)
+        def _():
+            load_x(k + 2).wait()
+            part[k + 2] = term(k + 2, 1 - c)
+            core_copy(k + 2).start()
+
+        core_copy(k).wait_recv()
+
+        @pl.when(k == 0)
+        def _():
+            send_z(0, 0, z_term(0, 0))
+            send_z(1, 0, z_term(0, 1))
+            send_x(0, 0)
+
+        @pl.when(k == 1)
+        def _():
+            send_z(0, 1, z_term(1, 0))
+            send_z(1, 1, z_term(1, 1))
+
+        @pl.when(k == 2)
+        def _():
+            send_x(1, 2)
+            send_z(0, 2, z_term(2, 1))
+            for dy in (1, 2, 3):
+                scatter_copy(dy).wait_recv()
+            half_sum[...] = mine[y_rows(0), :] + slots[0] + slots[1] + slots[2]
+            cross_copy().start()
+
+        @pl.when(k == 3)
+        def _():
+            send_z(1, 2, z_term(3, 0))
+            send_x(2, 3)
+            send_z(0, 3, z_plus(0, 2, 0))
+            send_z(1, 3, z_plus(1, 3, 0))
+
+        @pl.when(k == 4)
+        def _():
+            send_z(0, 4, z_term(4, 1))
+            cross_copy().wait_recv()
+            total[y_rows(0), :] = half_sum[...] + half_in[...]
+            for dy in (1, 2, 3):
+                gather_copy(dy).start()
+
+        @pl.when(k == 5)
+        def _():
+            send_z(1, 4, z_term(5, 0))
+            arrive(x_copy(0))
+            send_w(0, 0, w_term(1, 0, 0))
+            send_w(1, 0, w_term(1, 0, 1))
+            send_z(0, 5, z_plus(0, 4, 1))
+            send_z(1, 5, z_plus(1, 5, 1))
+
+        @pl.when(k == 6)
+        def _():
+            send_x(3, 6)
+            arrive(x_copy(1))
+            send_w(0, 1, w_term(4, 1, 1))
+
     for d in (0, 1):
         arrive(z_copy(d, 2))
         arrive(z_copy(d, 3))
@@ -286,8 +303,6 @@
         encode(z_sum(6, 2, 3, side), yq.at[:, columns], ys.at[:, columns])
     start(y_copy())
 
-    arrive(x_copy(1))
-    send_w(0, 1, w_term(4, 1, 1))
     arrive(x_copy(2))
     send_w(1, 1, w_term(5, 2, 0))
     for d, k, slot in ((0, 4, 1), (1, 5, 2)):
@@ -298,30 +313,28 @@
     for d in (0, 1):
         arrive(z_copy(d, 4))
         arrive(z_copy(d, 5))
+    for side in (0, 1):
+        collect(side, 0, zrows, z_sum(7, 4, 5, side))
     arrive(x_copy(3))
+    for d in (0, 1):
+        arrive(w_copy(d, 1))
+    for side in (0, 1):
+        base = w_term(7, 3, side)
+        collect(
+            side, zrows, wrows,
+            lambda lanes, side=side, base=base: base(lanes)
+            + decode(wq_in.at[1 - side, 1], ws_in.at[1 - side, 1], lanes),
+        )
+    for d in (0, 1):
+        arrive(w_copy(d, 2))
+    for side in (0, 1):
+        add(side, zrows, wrows, lambda lanes, side=side: decode(wq_in.at[side, 2], ws_in.at[side, 2], lanes))
     arrive(y_copy())
     for side in (0, 1):
-        base = z_sum(7, 4, 5, side)
-
-        @pl.loop(0, half // LANES)
-        def _(j):
-            lanes = pl.ds(pl.multiple_of(j * LANES, LANES), LANES)
-            grad[side, pl.ds(0, zrows), lanes] = base(lanes) + decode(yq_in, ys_in, shifted(lanes, side * half))
-
-    for d in (0, 1):
-        arrive(w_copy(d, 1))
-        arrive(w_copy(d, 2))
-    for side in (0, 1):
-        base = w_term(7, 3, side)
-
-        @pl.loop(0, half // LANES)
-        def _(j):
-            lanes = pl.ds(pl.multiple_of(j * LANES, LANES), LANES)
-            grad[side, pl.ds(zrows, wrows), lanes] = (
-                base(lanes)
-                + decode(wq_in.at[side, 2], ws_in.at[side, 2], lanes)
-                + decode(wq_in.at[1 - side, 1], ws_in.at[1 - side, 1], lanes)
-            )
+        add(side, 0, zrows, lambda lanes, side=side: decode(yq_in, ys_in, shifted(lanes, side * half)))
+
+    for copy in load_rest:
+        copy.wait()
 
     for dy in (1, 2, 3):
         gather_arrive(dy).wait_recv()
@@ -341,29 +354,50 @@
 
 
 def update_kernel(
-    islands, frag, grad, total, lw, first, second, anchor, moment, lw_out, first_out, second_out, anchor_out, moment_out
+    islands, step, frag, grad, total, lw, first, second, anchor, moment,
+    lw_out, first_out, second_out, anchor_out, moment_out, lw_new, first_new, second_new, anchor_new, moment_new, sems,
 ):
     index = frag[0]
+    rows = lw.shape[2]
     heads = lw.shape[3] // HEAD
-    proj, column = index // heads, pl.multiple_of(index % heads * HEAD, HEAD)
-    anchor_f = anchor[proj, :, pl.ds(column, HEAD)]
-    moment_f = moment[proj, :, pl.ds(column, HEAD)]
-    drift = anchor_f - total[...] * (1.0 / islands)
-    moment_new = 0.9 * moment_f + drift
-    merged = anchor_f - 0.7 * (0.9 * moment_new + drift)
-    for p in range(lw.shape[1]):
-        for j in range(heads):
-            here = index == p * heads + j
-            lanes = pl.ds(j * HEAD, HEAD)
-            anchor_out[p, :, lanes] = jnp.where(here, merged, anchor[p, :, lanes])
-            moment_out[p, :, lanes] = jnp.where(here, moment_new, moment[p, :, lanes])
-            begin = jnp.where(here, merged, lw[0, p, :, lanes])
-            g = grad[p, :, lanes]
-            m = 0.9 * first[0, p, :, lanes] + 0.1 * g
-            v = 0.95 * second[0, p, :, lanes] + 0.05 * g * g
-            first_out[0, p, :, lanes] = m
-            second_out[0, p, :, lanes] = v
-            lw_out[0, p, :, lanes] = begin - 0.02 * (m / (jnp.sqrt(v) + 1e-08) + 0.1 * begin)
+    groups = [(p, pl.ds(j * HEAD, HEAD)) for p in range(lw.shape[1]) for j in range(heads)]
+
+    def copies(i):
+        some = pl.ds(pl.multiple_of(i * step, step), step)
+        pairs = [(lw_new, lw_out.at[0]), (first_new, first_out.at[0]), (second_new, second_out.at[0])]
+        pairs += [(anchor_new, anchor_out), (moment_new, moment_out)]
+        return [
+            pltpu.make_async_copy(src.at[:, some], dst.at[:, some], sems.at[i, n]) for n, (src, dst) in enumerate(pairs)
+        ]
+
+    @pl.loop(0, rows // step)
+    def _(i):
+        some = pl.ds(pl.multiple_of(i * step, step), step)
+        anchor_f, moment_f = anchor[0, some, groups[0][1]], moment[0, some, groups[0][1]]
+        for g, (p, lanes) in enumerate(groups[1:], 1):
+            anchor_f = jnp.where(index == g, anchor[p, some, lanes], anchor_f)
+            moment_f = jnp.where(index == g, moment[p, some, lanes], moment_f)
+        drift = anchor_f - total[some, :] * (1.0 / islands)
+        moment_f = 0.9 * moment_f + drift
+        merged = anchor_f - 0.7 * (0.9 * moment_f + drift)
+        for g, (p, lanes) in enumerate(groups):
+            here = index == g
+            anchor_new[p, some, lanes] = jnp.where(here, merged, anchor[p, some, lanes])
+            moment_new[p, some, lanes] = jnp.where(here, moment_f, moment[p, some, lanes])
+            begin = jnp.where(here, merged, lw[0, p, some, lanes])
+            gr = grad[p, some, lanes]
+            m = 0.9 * first[0, p, some, lanes] + 0.1 * gr
+            v = 0.95 * second[0, p, some, lanes] + 0.05 * gr * gr
+            first_new[p, some, lanes] = m
+            second_new[p, some, lanes] = v
+            lw_new[p, some, lanes] = begin - 0.02 * (m / (jnp.sqrt(v) + 1e-08) + 0.1 * begin)
+        for copy in copies(i):
+            copy.start()
+
+    @pl.loop(0, rows // step)
+    def _(i):
+        for copy in copies(i):
+            copy.wait()
 
 
 def body(features, upstream, local_weights, first_moment, second_moment, anchor, outer_momentum, fragment):
@@ -383,19 +417,16 @@
     def sems(*shape):
         return pltpu.SemaphoreType.DMA(shape)
 
+    states = (local_weights, first_moment, second_moment, anchor, outer_momentum)
     any_space = pl.BlockSpec(memory_space=pl.ANY)
-    grad, total = pl.pallas_call(
+    near = pl.pallas_call(
         functools.partial(grad_kernel, rows, zrows),
-        out_shape=(
-            jax.ShapeDtypeStruct((frags, rows, half), F32),
-            jax.ShapeDtypeStruct((rows, HEAD), F32),
-        ),
-        in_specs=[any_space, any_space, any_space, pl.BlockSpec(memory_space=pltpu.SMEM)],
-        out_specs=(pl.BlockSpec(memory_space=pltpu.VMEM), pl.BlockSpec(memory_space=pltpu.VMEM)),
+        out_shape=(vm((frags, rows, half), F32), vm((rows, HEAD), F32), *[vm(a.shape, F32) for a in states]),
+        in_specs=[any_space] * 7 + [pl.BlockSpec(memory_space=pltpu.SMEM)],
+        out_specs=[pl.BlockSpec(memory_space=pltpu.VMEM)] * 7,
         scratch_shapes=[
             vm((tokens, width), jnp.bfloat16),
             vm((tokens, cols), jnp.bfloat16),
-            vm((frags, rows, half), F32),
             vm((8, rows, cols), F32),
             vm((8, rows, cols), F32),
             vm((8, rows, cols), F32),
@@ -407,7 +438,7 @@
             vm((3, rows // 4, HEAD), F32),
             vm((rows // 4, HEAD), F32),
             vm((rows // 4, HEAD), F32),
-            sems(10),
+            sems(14),
             sems(8),
             sems(8),
             sems(2, 6, 2),
@@ -422,32 +453,21 @@
             sems(7),
         ],
         compiler_params=pltpu.CompilerParams(
-            collective_id=0, has_side_effects=True, vmem_limit_bytes=56 * 2**20
+            collective_id=0, has_side_effects=True, vmem_limit_bytes=48 * 2**20
         ),
-    )(features, upstream, local_weights, fragment)
-
-    step = rows // 4
-    state = pl.BlockSpec((1, frags, step, half), lambda i: (0, 0, i, 0))
-    shared = pl.BlockSpec((frags, step, half), lambda i: (0, i, 0))
+    )(features, upstream, *states, fragment)
+
+    step = rows // 8
     weights_shape = jax.ShapeDtypeStruct(local_weights.shape, F32)
     anchor_shape = jax.ShapeDtypeStruct(anchor.shape, F32)
     return pl.pallas_call(
-        functools.partial(update_kernel, lax.axis_size("island")),
-        grid=(4,),
+        functools.partial(update_kernel, lax.axis_size("island"), step),
         out_shape=(weights_shape, weights_shape, weights_shape, anchor_shape, anchor_shape),
-        in_specs=[
-            pl.BlockSpec(memory_space=pltpu.SMEM),
-            shared,
-            pl.BlockSpec((step, HEAD), lambda i: (i, 0)),
-            state,
-            state,
-            state,
-            shared,
-            shared,
-        ],
-        out_specs=(state, state, state, shared, shared),
+        in_specs=[pl.BlockSpec(memory_space=pltpu.SMEM)] + [pl.BlockSpec(memory_space=pltpu.VMEM)] * 7,
+        out_specs=[any_space] * 5,
+        scratch_shapes=[vm((frags, rows, half), F32)] * 5 + [sems(8, 5)],
         compiler_params=pltpu.CompilerParams(vmem_limit_bytes=16 * 2**20),
-    )(fragment, grad, total, local_weights, first_moment, second_moment, anchor, outer_momentum)
+    )(fragment, *[pltpu.with_memory_space_constraint(a, pltpu.VMEM) for a in near])
 
 
 def solution(mesh):

time: 53.3 us -> 45.1 us (0.85); the launches traced: 52.4 us -> 45 us
  Pallas kernels: 48.7 us -> 43.7 us
  local copies, waits for them, and re-layouts: 2.14 us -> 0 us
    pallas_call x2, Pallas kernels: 48.7 us -> 43.7 us  [the longest x1 40.9 us: body(): pl.pallas_call(functools.partial(grad_kernel, rows, zrows), out_shape=(vm...]
    unnamed x14 -> x0, local copies, waits for them, and re-layouts: 2.14 us -> none
where the time goes in v2:
time: 45.1 us; the launch traced here: 45 us
  Pallas kernels  43.7 us (97%)
  between operations  1.29 us (3%)
    pallas_call x1, Pallas kernels, body(): pl.pallas_call(functools.partial(grad_kernel, rows, zrows), out_shape=(vm...  40.9 us
    pallas_call x1, Pallas kernels, body(): pl.pallas_call(functools.partial(update_kernel, lax.axis_size('island'),...  2.79 us

profile of v2, /device:TPU:0, one launch (start us, length us, event | category | flops | bytes accessed | tf_op | source)
XLA Modules:
  0.0 45.0 jit_solution(6955783971621727067)
XLA Ops:
  1.3 40.9 %shard_map.119 = (f32[2,256,512]{2,1,0:T(8,128)S(1)}, f32[256,128]{1,0:T(8,128)S(1)}, f32[1,2,256,512]{3,2,1,0:T(8,128)S(1)}, f32[1,2,256,512]{3,2,1,0:T(8,128)S...) custom-call(bf16[1,1024,4096]{2,1,0:T(8,128)(2,1)} %x_hbm.1, ...), custom_call_target="tpu_custom_call" | custom-call | tf_op jit(solution)/shard_map/pallas_call | solution.py:422
  42.2 2.8 %shard_map.120 = (f32[1,2,256,512]{3,2,1,0:T(8,128)}, f32[1,2,256,512]{3,2,1,0:T(8,128)}, f32[1,2,256,512]{3,2,1,0:T(8,128)}, f32[2,256,512]{2,1,0:T(8,128)}, f32[2,256,512]{2,1,0:T(8,128)}) custom-call(s32[1]{0:T(128)S(6)} %copy.13.frag, f32[2,256,512]{2,1,0:T(8,128)S(1)} %get-tuple-element.12.grad, f32[256,128]{1,0:T(8,128)S(1)} %get-tuple-element.13.total, ...), custom_call_target="tpu_custom_call" | custom-call | tf_op jit(solution)/shard_map/pallas_call | solution.py:463

commit v3 on v2

v3 whole, which is shorter than its diff:
```python
import functools

import jax
import jax.numpy as jnp
from jax import lax
from jax.experimental import pallas as pl
from jax.experimental.pallas import tpu as pltpu
from jax.sharding import PartitionSpec as P

HEAD = 128
LANES = 128
TOP = 32766.0
TINY = 1e-30
F32 = jnp.float32
MESH = pl.DeviceIdType.MESH


def encode(value, codes, scales):
    @pl.loop(0, codes.shape[1] // LANES)
    def _(j):
        lanes = pl.ds(pl.multiple_of(j * LANES, LANES), LANES)
        v = value(lanes)
        top = jnp.maximum(jnp.max(jnp.abs(v), axis=0, keepdims=True), TINY)
        scales[:, lanes] = top * (1.0 / TOP)
        codes[:, lanes] = jnp.round(v * (TOP / top)).astype(jnp.int32).astype(jnp.int16)


def decode(codes, scales, lanes):
    return codes[:, lanes].astype(jnp.int32).astype(F32) * scales[:, lanes]


def grad_kernel(
    islands, rows, zrows, x_hbm, u_hbm, lw_hbm, first_hbm, second_hbm, anchor_hbm, moment_hbm, frag,
    grad, lwb, firstb, secondb, anchorb, momentb,
    xb, ub, part, own, core_in,
    zq, zs, zq_in, zs_in, wq, ws, wq_in, ws_in,
    xq, xs, xq_in, xs_in, yq, ys, yq_in, ys_in,
    mine, slots, half_sum, half_in, total,
    load_sem, state_sem, core_ss, core_rs, z_ss, z_rs, w_ss, w_rs, x_ss, x_rs, y_ss, y_rs, d_ss, d_rs,
):
    isl, place = lax.axis_index("island"), lax.axis_index("fsdp")
    z, x, c = place // 4, place // 2 % 2, place % 2
    y, h = isl // 2, isl % 2
    half = grad.shape[2]
    quarter = rows // 4

    def at(dz=0, dx=0, dc=0):
        return (isl, (z + dz) % 4 * 4 + (x + dx) % 2 * 2 + (c + dc) % 2)

    def island(dy=0, dh=0):
        return ((y + dy) % 4 * 2 + (h + dh) % 2, place)

    def order(k):
        dz = jnp.where(k < 2, 2, jnp.where(k >= 6, 0, jnp.where(k % 2 == 0, 1, 3)))
        dx = jnp.where(k < 2, 1 - k, jnp.where(k < 4, 1, jnp.where(k < 6, 0, 7 - k)))
        return (z + dz) % 4 * 2 + (x + dx) % 2

    def block(k, core):
        return pl.ds(pl.multiple_of((order(k) * 2 + core) * rows, rows), rows)

    def load_x(k, core):
        columns = block(k, (c + core) % 2)
        return pltpu.make_async_copy(x_hbm.at[0, :, columns], xb.at[:, columns], load_sem.at[k, core])

    def load_u(side):
        columns = pl.ds(side * half, half)
        return pltpu.make_async_copy(u_hbm.at[0, :, columns], ub.at[:, columns], load_sem.at[8, side])

    states = ((lw_hbm, lwb), (first_hbm, firstb), (second_hbm, secondb), (anchor_hbm, anchorb), (moment_hbm, momentb))
    load_states = [pltpu.make_async_copy(src, dst, state_sem.at[n]) for n, (src, dst) in enumerate(states)]
    load_u(0).start()
    load_x(0, 1).start()
    load_u(1).start()
    load_x(0, 0).start()

    barrier = pltpu.get_barrier_semaphore()
    peers = [at(dc=1), at(dx=1), at(dz=1), at(dz=3), island(1), island(2), island(3), island(dh=1)]
    for peer in peers:
        pl.semaphore_signal(barrier, inc=1, device_id=peer, device_id_type=MESH)

    def remote(src, dst, ss, rs, peer):
        return pltpu.make_async_remote_copy(
            src_ref=src, dst_ref=dst, send_sem=ss, recv_sem=rs, device_id=peer, device_id_type=MESH
        )

    def term(k, core, side=None):
        columns = pl.ds(0, 2 * half) if side is None else pl.ds(side * half, half)
        return lax.dot_general(
            xb[:, block(k, core)], ub[:, columns], (((0,), (0,)), ((), ())), preferred_element_type=F32
        )

    def store(terms, k, value):
        for side in (0, 1):
            terms[k, side] = value[:, side * half : (side + 1) * half]

    def core_copy(k, side):
        return remote(part.at[k, side], core_in.at[k, side], core_ss.at[k, side], core_rs.at[k, side], at(dc=1))

    def z_copy(d, s):
        peer = at(dz=1 if d == 0 else 3)
        return (
            remote(zq.at[d, s], zq_in.at[d, s], z_ss.at[d, s, 0], z_rs.at[d, s, 0], peer),
            remote(zs.at[d, s], zs_in.at[d, s], z_ss.at[d, s, 1], z_rs.at[d, s, 1], peer),
        )

    def w_copy(d, s):
        peer = at(dz=1 if d == 0 else 3)
        return (
            remote(wq.at[d, s], wq_in.at[d, s], w_ss.at[d, s, 0], w_rs.at[d, s, 0], peer),
            remote(ws.at[d, s], ws_in.at[d, s], w_ss.at[d, s, 1], w_rs.at[d, s, 1], peer),
        )

    def x_copy(s, side):
        peer = at(dx=1)
        return (
            remote(xq.at[s, side], xq_in.at[s, side], x_ss.at[s, side, 0], x_rs.at[s, side, 0], peer),
            remote(xs.at[s, side], xs_in.at[s, side], x_ss.at[s, side, 1], x_rs.at[s, side, 1], peer),
        )

    def y_copy(side):
        peer = at(dx=1)
        return (
            remote(yq.at[side], yq_in.at[side], y_ss.at[side, 0], y_rs.at[side, 0], peer),
            remote(ys.at[side], ys_in.at[side], y_ss.at[side, 1], y_rs.at[side, 1], peer),
        )

    def start(pair):
        for copy in pair:
            copy.start()

    def arrive(pair):
        for copy in pair:
            copy.wait_recv()

    def chip_term(k, r, n, side):
        return lambda lanes: own[k, side, pl.ds(r, n), lanes] + core_in[k, side, pl.ds(r, n), lanes]

    wrows = rows - zrows

    def z_term(k, side):
        return chip_term(k, 0, zrows, side)

    def w_term(k, slot, side):
        base = chip_term(k, zrows, wrows, side)

        return lambda lanes: base(lanes) + decode(xq_in.at[slot, side], xs_in.at[slot, side], lanes)

    def send_z(d, s, value):
        encode(value, zq.at[d, s], zs.at[d, s])
        start(z_copy(d, s))

    def send_w(d, s, value):
        encode(value, wq.at[d, s], ws.at[d, s])
        start(w_copy(d, s))

    def send_x(s, k, side):
        encode(chip_term(k, zrows, wrows, side), xq.at[s, side], xs.at[s, side])
        start(x_copy(s, side))

    def z_plus(d, k, got):
        arrive(z_copy(d, got))
        return lambda lanes: z_term(k, d)(lanes) + decode(zq_in.at[d, got], zs_in.at[d, got], lanes)

    load_x(0, 1).wait()
    for side in (0, 1):
        load_u(side).wait()
        part[0, side] = term(0, 1 - c, side)
        if side == 0:
            pl.semaphore_wait(barrier, len(peers))
        core_copy(0, side).start()

    for k in (1, 2):
        load_x(k, 1).start()
        load_x(k, 0).start()
    load_states[0].start()
    load_x(0, 0).wait()
    store(own, 0, term(0, c))
    for side in (0, 1):
        core_copy(0, side).wait_recv()
        send_z(side, 0, z_term(0, side))
        send_x(0, 0, side)

    @pl.loop(3, 8)
    def _(k):
        load_x(k, 1).start()
        load_x(k, 0).start()

    load_x(1, 1).wait()
    store(part, 1, term(1, 1 - c))
    for side in (0, 1):
        core_copy(1, side).start()

    load_states[0].wait()
    index = frag[0]
    heads = half // HEAD
    groups = [(p, pl.ds(j * HEAD, HEAD)) for p in range(lwb.shape[1]) for j in range(heads)]

    def fragment(array, few):
        chosen = array[0, few, groups[0][1]]
        for g, (p, lanes) in enumerate(groups[1:], 1):
            chosen = jnp.where(index == g, array[p, few, lanes], chosen)
        return chosen

    def by_rows(body):
        @pl.loop(0, rows // 32)
        def _(j):
            body(pl.ds(pl.multiple_of(j * 32, 32), 32))

    @by_rows
    def _(few):
        mine[few, :] = fragment(lwb.at[0], few)

    def y_rows(dy):
        return pl.ds(pl.multiple_of((y + dy) % 4 * quarter, quarter), quarter)

    def scatter_copy(dy):
        return remote(mine.at[y_rows(dy)], slots.at[dy - 1], d_ss.at[dy - 1], d_rs.at[dy - 1], island(dy))

    def cross_copy():
        return remote(half_sum, half_in, d_ss.at[3], d_rs.at[3], island(dh=1))

    def gather_copy(dy):
        return remote(total.at[y_rows(0)], total.at[y_rows(0)], d_ss.at[3 + dy], d_rs.at[3 + dy], island(dy))

    def gather_arrive(dy):
        rows_in = total.at[y_rows(-dy)]
        return remote(rows_in, rows_in, d_ss.at[3 + dy], d_rs.at[3 + dy], island(dy))

    for dy in (1, 2, 3):
        scatter_copy(dy).start()
    for copy in load_states[1:]:
        copy.start()

    def z_sum(k, leaf, chain, side):
        def value(lanes):
            return (
                z_term(k, side)(lanes)
                + decode(zq_in.at[side, chain], zs_in.at[side, chain], lanes)
                + decode(zq_in.at[1 - side, leaf], zs_in.at[1 - side, leaf], lanes)
            )

        return value

    def collect(side, r, n, value):
        @pl.loop(0, half // LANES)
        def _(j):
            lanes = pl.ds(pl.multiple_of(j * LANES, LANES), LANES)
            grad[side, pl.ds(r, n), lanes] = value(lanes)

    def add(side, r, n, value):
        @pl.loop(0, half // LANES)
        def _(j):
            lanes = pl.ds(pl.multiple_of(j * LANES, LANES), LANES)
            grad[side, pl.ds(r, n), lanes] += value(lanes)

    @pl.loop(1, 8)
    def _(k):
        @pl.when(k < 7)
        def _():
            load_x(k + 1, 1).wait()
            store(part, k + 1, term(k + 1, 1 - c))
            for side in (0, 1):
                core_copy(k + 1, side).start()

        load_x(k, 0).wait()
        store(own, k, term(k, c))
        for side in (0, 1):
            core_copy(k, side).wait_recv()

        @pl.when(k == 1)
        def _():
            send_z(0, 1, z_term(1, 0))
            send_z(1, 1, z_term(1, 1))

        @pl.when(k == 2)
        def _():
            send_z(0, 2, z_term(2, 1))
            send_x(1, 2, 0)
            send_x(1, 2, 1)

        @pl.when(k == 3)
        def _():
            send_z(1, 2, z_term(3, 0))
            for dy in (1, 2, 3):
                scatter_copy(dy).wait_recv()
            half_sum[...] = mine[y_rows(0), :] + slots[0] + slots[1] + slots[2]
            cross_copy().start()
            send_x(2, 3, 0)
            send_x(2, 3, 1)
            send_z(0, 3, z_plus(0, 2, 0))
            send_z(1, 3, z_plus(1, 3, 0))

        @pl.when(k == 4)
        def _():
            send_z(0, 4, z_term(4, 1))

        @pl.when(k == 5)
        def _():
            send_z(1, 4, z_term(5, 0))
            for d in (0, 1):
                arrive(x_copy(0, d))
                send_w(d, 0, w_term(1, 0, d))
            send_z(0, 5, z_plus(0, 4, 1))
            send_z(1, 5, z_plus(1, 5, 1))

        @pl.when(k == 6)
        def _():
            send_x(3, 6, 0)
            send_x(3, 6, 1)
            arrive(x_copy(1, 0))
            arrive(x_copy(1, 1))
            send_w(0, 1, w_term(4, 1, 1))

    for d in (0, 1):
        arrive(z_copy(d, 2))
        arrive(z_copy(d, 3))
    for side in (0, 1):
        encode(z_sum(6, 2, 3, side), yq.at[side], ys.at[side])
        start(y_copy(side))

    cross_copy().wait_recv()
    total[y_rows(0), :] = half_sum[...] + half_in[...]
    for dy in (1, 2, 3):
        gather_copy(dy).start()

    arrive(x_copy(2, 0))
    arrive(x_copy(2, 1))
    send_w(1, 1, w_term(5, 2, 0))
    for d, k, slot in ((0, 4, 1), (1, 5, 2)):
        arrive(w_copy(d, 0))
        base = w_term(k, slot, d)
        send_w(d, 2, lambda lanes, d=d, base=base: base(lanes) + decode(wq_in.at[d, 0], ws_in.at[d, 0], lanes))

    for dy in (1, 2, 3):
        gather_arrive(dy).wait_recv()
    for copy in load_states[1:]:
        copy.wait()

    @by_rows
    def _(few):
        anchor_f = fragment(anchorb, few)
        drift = anchor_f - total[few, :] * (1.0 / islands)
        moment_f = 0.9 * fragment(momentb, few) + drift
        merged = anchor_f - 0.7 * (0.9 * moment_f + drift)
        for g, (p, lanes) in enumerate(groups):
            here = index == g
            anchorb[p, few, lanes] = jnp.where(here, merged, anchorb[p, few, lanes])
            momentb[p, few, lanes] = jnp.where(here, moment_f, momentb[p, few, lanes])
            lwb[0, p, few, lanes] = jnp.where(here, merged, lwb[0, p, few, lanes])

    for d in (0, 1):
        arrive(z_copy(d, 4))
        arrive(z_copy(d, 5))
    for side in (0, 1):
        collect(side, 0, zrows, z_sum(7, 4, 5, side))
    arrive(x_copy(3, 0))
    arrive(x_copy(3, 1))
    for d in (0, 1):
        arrive(w_copy(d, 1))
    for side in (0, 1):
        base = w_term(7, 3, side)
        collect(
            side, zrows, wrows,
            lambda lanes, side=side, base=base: base(lanes)
            + decode(wq_in.at[1 - side, 1], ws_in.at[1 - side, 1], lanes),
        )
    def finish(pairs):
        for pair in pairs:
            for copy in pair:
                copy.wait_send()

    finish([[scatter_copy(dy), gather_copy(dy)] for dy in (1, 2, 3)] + [[cross_copy()]])

    @pl.loop(0, 8)
    def _(k):
        finish([[core_copy(k, side) for side in (0, 1)]])

    finish([z_copy(d, s) for d in (0, 1) for s in range(6)] + [w_copy(d, s) for d in (0, 1) for s in (0, 1)])
    finish([x_copy(s, side) for s in range(4) for side in (0, 1)])

    for d in (0, 1):
        arrive(w_copy(d, 2))
    for side in (0, 1):
        add(side, zrows, wrows, lambda lanes, side=side: decode(wq_in.at[side, 2], ws_in.at[side, 2], lanes))
    for side in (0, 1):
        arrive(y_copy(side))
        add(side, 0, zrows, lambda lanes, side=side: decode(yq_in.at[side], ys_in.at[side], lanes))

    finish([w_copy(d, 2) for d in (0, 1)] + [y_copy(side) for side in (0, 1)])


def update_kernel(
    step, grad, lw, first, second, anchor, moment,
    lw_out, first_out, second_out, anchor_out, moment_out, lw_new, first_new, second_new, sems, shared_sems,
):
    shared = [
        pltpu.make_async_copy(src, dst, shared_sems.at[n])
        for n, (src, dst) in enumerate(((anchor, anchor_out), (moment, moment_out)))
    ]
    for copy in shared:
        copy.start()
    frags, rows, half = grad.shape
    groups = [(p, pl.ds(j * LANES, LANES)) for p in range(frags) for j in range(half // LANES)]

    def copies(i):
        some = pl.ds(pl.multiple_of(i * step, step), step)
        pairs = [(lw_new, lw_out.at[0]), (first_new, first_out.at[0]), (second_new, second_out.at[0])]
        return [
            pltpu.make_async_copy(src.at[:, some], dst.at[:, some], sems.at[i, n]) for n, (src, dst) in enumerate(pairs)
        ]

    @pl.loop(0, rows // step)
    def _(i):
        some = pl.ds(pl.multiple_of(i * step, step), step)
        for p, lanes in groups:
            gr = grad[p, some, lanes]
            begin = lw[0, p, some, lanes]
            m = 0.9 * first[0, p, some, lanes] + 0.1 * gr
            v = 0.95 * second[0, p, some, lanes] + 0.05 * gr * gr
            first_new[p, some, lanes] = m
            second_new[p, some, lanes] = v
            lw_new[p, some, lanes] = begin - 0.02 * (m / (jnp.sqrt(v) + 1e-08) + 0.1 * begin)
        for copy in copies(i):
            copy.start()

    @pl.loop(0, rows // step)
    def _(i):
        for copy in copies(i):
            copy.wait()

    for copy in shared:
        copy.wait()


def body(features, upstream, local_weights, first_moment, second_moment, anchor, outer_momentum, fragment):
    _, tokens, width = features.shape
    _, frags, rows, half = local_weights.shape
    cols = frags * half
    zrows = rows * 9 // 16
    wrows = rows - zrows
    i16 = jnp.int16

    def vm(shape, dtype):
        return pltpu.VMEM(shape, dtype)

    def both(*shape):
        return [vm(shape, i16), vm(shape[:-2] + (1, shape[-1]), F32)] * 2

    def sems(*shape):
        return pltpu.SemaphoreType.DMA(shape)

    states = (local_weights, first_moment, second_moment, anchor, outer_momentum)
    any_space = pl.BlockSpec(memory_space=pl.ANY)
    near = pl.pallas_call(
        functools.partial(grad_kernel, lax.axis_size("island"), rows, zrows),
        out_shape=(vm((frags, rows, half), F32), *[vm(a.shape, F32) for a in states]),
        in_specs=[any_space] * 7 + [pl.BlockSpec(memory_space=pltpu.SMEM)],
        out_specs=[pl.BlockSpec(memory_space=pltpu.VMEM)] * 6,
        scratch_shapes=[
            vm((tokens, width), jnp.bfloat16),
            vm((tokens, cols), jnp.bfloat16),
            vm((8, frags, rows, half), F32),
            vm((8, frags, rows, half), F32),
            vm((8, frags, rows, half), F32),
            *both(2, 6, zrows, half),
            *both(2, 3, wrows, half),
            *both(4, 2, wrows, half),
            *both(2, zrows, half),
            vm((rows, HEAD), F32),
            vm((3, rows // 4, HEAD), F32),
            vm((rows // 4, HEAD), F32),
            vm((rows // 4, HEAD), F32),
            vm((rows, HEAD), F32),
            sems(9, 2),
            sems(5),
            sems(8, 2),
            sems(8, 2),
            sems(2, 6, 2),
            sems(2, 6, 2),
            sems(2, 3, 2),
            sems(2, 3, 2),
            sems(4, 2, 2),
            sems(4, 2, 2),
            sems(2, 2),
            sems(2, 2),
            sems(7),
            sems(7),
        ],
        compiler_params=pltpu.CompilerParams(
            collective_id=0, has_side_effects=True, vmem_limit_bytes=48 * 2**20
        ),
    )(features, upstream, *states, fragment)

    step = rows // 8
    weights_shape = jax.ShapeDtypeStruct(local_weights.shape, F32)
    anchor_shape = jax.ShapeDtypeStruct(anchor.shape, F32)
    return pl.pallas_call(
        functools.partial(update_kernel, step),
        out_shape=(weights_shape, weights_shape, weights_shape, anchor_shape, anchor_shape),
        in_specs=[pl.BlockSpec(memory_space=pltpu.VMEM)] * 6,
        out_specs=[any_space] * 5,
        scratch_shapes=[vm((frags, rows, half), F32)] * 3 + [sems(8, 3), sems(2)],
        compiler_params=pltpu.CompilerParams(vmem_limit_bytes=16 * 2**20),
    )(*[pltpu.with_memory_space_constraint(a, pltpu.VMEM) for a in near])


def solution(mesh):
    placed = (
        P("island", "fsdp", None),
        P("island", "fsdp", None),
        P("island", None, "fsdp", None),
        P("island", None, "fsdp", None),
        P("island", None, "fsdp", None),
        P(None, "fsdp", None),
        P(None, "fsdp", None),
        P(),
    )
    return jax.shard_map(
        body,
        mesh=mesh,
        in_specs=placed,
        out_specs=(
            P("island", None, "fsdp", None),
            P("island", None, "fsdp", None),
            P("island", None, "fsdp", None),
            P(None, "fsdp", None),
            P(None, "fsdp", None),
        ),
        check_vma=False,
    )
```

time: 45.1 us -> 43.5 us (0.965)
  Pallas kernels: 43.7 us -> 42.1 us
    pallas_call x2, Pallas kernels: 43.7 us -> 42.1 us  [the longest x1 39.6 us: body(): pl.pallas_call(functools.partial(grad_kernel, lax.axis_size('island'), ro...]
where the time goes in v3:
time: 43.5 us; the launch traced here: 43.4 us
  Pallas kernels  42.1 us (97%)
  between operations  1.29 us (3%)
    pallas_call x1, Pallas kernels, body(): pl.pallas_call(functools.partial(grad_kernel, lax.axis_size('island'), ro...  39.6 us
    pallas_call x1, Pallas kernels, body(): pl.pallas_call(functools.partial(update_kernel, step), out_shape=(weights...  2.54 us

profile of v3, /device:TPU:0, one launch (start us, length us, event | category | flops | bytes accessed | tf_op | source)
XLA Modules:
  0.0 43.4 jit_solution(4042542388012072345)
XLA Ops:
  1.3 39.6 %shard_map.119 = (f32[2,256,512]{2,1,0:T(8,128)S(1)}, f32[1,2,256,512]{3,2,1,0:T(8,128)S(1)}, f32[1,2,256,512]{3,2,1,0:T(8,128)S(1)}, f32[1,2,256,512]{3,2,1,0:T...) custom-call(bf16[1,1024,4096]{2,1,0:T(8,128)(2,1)} %x_hbm.1, bf16[1,1024,1024]{2,1,0:T(8,128)(2,1)} %u_hbm.1, ...), custom_call_target="tpu_custom_call" | custom-call | tf_op jit(solution)/shard_map/pallas_call | solution.py:454
  40.9 2.5 %shard_map.120 = (f32[1,2,256,512]{3,2,1,0:T(8,128)}, f32[1,2,256,512]{3,2,1,0:T(8,128)}, f32[1,2,256,512]{3,2,1,0:T(8,128)}, f32[2,256,512]{2,1,0:T(8,128)}, f32[2,256,512]{2,1,0:T(8,128)}) custom-call(f32[2,256,512]{2,1,0:T(8,128)S(1)} %get-tuple-element.11.grad, f32[1,2,256,512]{3,2,1,0:T(8,128)S(1)} %get-tuple-element.12.lw, ...), custom_call_target="tpu_custom_call" | custom-call | tf_op jit(solution)/shard_map/pallas_call | solution.py:497

commit v4 on v3

--- a/solution.py
+++ b/solution.py
@@ -11,6 +11,7 @@
 LANES = 128
 TOP = 32766.0
 TINY = 1e-30
+LIMIT = 6.0
 F32 = jnp.float32
 MESH = pl.DeviceIdType.MESH
 
@@ -43,6 +44,7 @@
     y, h = isl // 2, isl % 2
     half = grad.shape[2]
     quarter = rows // 4
+    reach = 4 * LIMIT
 
     def at(dz=0, dx=0, dc=0):
         return (isl, (z + dz) % 4 * 4 + (x + dx) % 2 * 2 + (c + dc) % 2)
@@ -283,7 +285,8 @@
             send_z(1, 2, z_term(3, 0))
             for dy in (1, 2, 3):
                 scatter_copy(dy).wait_recv()
-            half_sum[...] = mine[y_rows(0), :] + slots[0] + slots[1] + slots[2]
+            column = mine[y_rows(0), :] + slots[0] + slots[1] + slots[2]
+            half_sum[...] = jnp.round(column * (TOP / reach)).astype(jnp.int32).astype(jnp.int16)
             cross_copy().start()
             send_x(2, 3, 0)
             send_x(2, 3, 1)
@@ -319,7 +322,7 @@
         start(y_copy(side))
 
     cross_copy().wait_recv()
-    total[y_rows(0), :] = half_sum[...] + half_in[...]
+    total[y_rows(0), :] = (half_sum[...].astype(jnp.int32) + half_in[...].astype(jnp.int32)).astype(F32) * (reach / TOP)
     for dy in (1, 2, 3):
         gather_copy(dy).start()
 
@@ -468,8 +471,8 @@
             *both(2, zrows, half),
             vm((rows, HEAD), F32),
             vm((3, rows // 4, HEAD), F32),
-            vm((rows // 4, HEAD), F32),
-            vm((rows // 4, HEAD), F32),
+            vm((rows // 4, HEAD), i16),
+            vm((rows // 4, HEAD), i16),
             vm((rows, HEAD), F32),
             sems(9, 2),
             sems(5),

time: 43.5 us -> 43.5 us (level)
  no operation moved by 1% of the time
where the time goes in v4:
time: 43.5 us; the launch traced here: 43.4 us
  Pallas kernels  42.1 us (97%)
  between operations  1.29 us (3%)
    pallas_call x1, Pallas kernels, body(): pl.pallas_call(functools.partial(grad_kernel, lax.axis_size('island'), ro...  39.6 us
    pallas_call x1, Pallas kernels, body(): pl.pallas_call(functools.partial(update_kernel, step), out_shape=(weights...  2.54 us

profile of v4, /device:TPU:0, one launch (start us, length us, event | category | flops | bytes accessed | tf_op | source)
XLA Modules:
  0.0 43.4 jit_solution(12086212977620599150)
XLA Ops:
  1.3 39.6 %shard_map.119 = (f32[2,256,512]{2,1,0:T(8,128)S(1)}, f32[1,2,256,512]{3,2,1,0:T(8,128)S(1)}, f32[1,2,256,512]{3,2,1,0:T(8,128)S(1)}, f32[1,2,256,512]{3,2,1,0:T...) custom-call(bf16[1,1024,4096]{2,1,0:T(8,128)(2,1)} %x_hbm.1, bf16[1,1024,1024]{2,1,0:T(8,128)(2,1)} %u_hbm.1, ...), custom_call_target="tpu_custom_call" | custom-call | tf_op jit(solution)/shard_map/pallas_call | solution.py:457
  40.9 2.5 %shard_map.120 = (f32[1,2,256,512]{3,2,1,0:T(8,128)}, f32[1,2,256,512]{3,2,1,0:T(8,128)}, f32[1,2,256,512]{3,2,1,0:T(8,128)}, f32[2,256,512]{2,1,0:T(8,128)}, f32[2,256,512]{2,1,0:T(8,128)}) custom-call(f32[2,256,512]{2,1,0:T(8,128)S(1)} %get-tuple-element.11.grad, f32[1,2,256,512]{3,2,1,0:T(8,128)S(1)} %get-tuple-element.12.lw, ...), custom_call_target="tpu_custom_call" | custom-call | tf_op jit(solution)/shard_map/pallas_call | solution.py:500
